TPU v7x, 512 devices: a whole 4x8x8 slice. The times are simulated.
512 devices in a mesh: row: 32 (over y_lo, z, core), col: 16 (over y_hi, x).
Axes of the slice: x: 4, y: 8 (y_hi: 4, y_lo: 2; y = y_hi * 2 + y_lo), z: 8, core: 2. Of those that a mesh axis runs over, the one named last changes fastest.
Arguments:
- tokens: bfloat16 [256, 512, 256], P('row', 'col'), may hold values from -6 to 6
- fine_proj: bfloat16 [256, 768], replicated, may hold values from -0.375 to 0.375
- fine_scale: float32 [4], replicated, may hold values from 3 to 12
- coarse_proj: bfloat16 [3, 1024, 1024], P(None, None, 'col'), may hold values from -0.1875 to 0.1875
- coarse_scale: float32 [16], P('col'), may hold values from 12 to 40
- coarse_cot: bfloat16 [32, 64, 1024], P('row', None, 'col'), may hold values from -6 to 6
Outputs:
- coarse_out: float32 [32, 64, 1024], P('row', None, 'col')
- fine_grad: bfloat16 [256, 512, 256], P('row', 'col')
All inputs are finite; a program needn't handle non-finite values.
Results may differ from a plain program's by a relative error of at most 0.035.
Values may be sent and summed in bfloat16 or wider, within the bound.
A program may use at most 64 MiB of HBM per device.

v0:
```python
from functools import partial

import jax
import jax.numpy as jnp
from jax import lax
from jax.sharding import PartitionSpec as P

epsilon = 1e-06


def padded_2(cells, sides, width):
    for axis, dim in sides:
        count = lax.axis_size(axis)
        ends = count - 1
        head = lax.slice_in_dim(cells, 0, width, axis=dim)
        tail = lax.slice_in_dim(cells, cells.shape[dim] - width, cells.shape[dim], axis=dim)
        cells = jnp.concatenate(
            [
                lax.ppermute(tail, axis, [(i, (i + 1) % count) for i in range(ends)]),
                cells,
                lax.ppermute(head, axis, [((i + 1) % count, i) for i in range(ends)]),
            ],
            axis=dim,
        )
    return cells


def shifted(value, axis, steps):
    count = lax.axis_size(axis)
    first, last = (max(0, -steps), min(count, count - steps))
    return lax.ppermute(value, axis, [(source, source + steps) for source in range(first, last)])


def unit_rows(tensor, scales):
    inverse = lax.rsqrt(jnp.sum(tensor * tensor, axis=-1, keepdims=True) + epsilon)
    return tensor * inverse * scales[:, None]


def rms_norm(field):
    return field * lax.rsqrt(jnp.mean(field * field, axis=-1, keepdims=True) + epsilon)


def merge_cells(field):
    height, breadth, width = field.shape
    grouped = field.reshape(height // 8, 2, 4, breadth // 8, 2, 4, width)
    pooled = jnp.mean(grouped, axis=(2, 5))
    return jnp.transpose(pooled, (0, 2, 1, 3, 4)).reshape(height // 8, breadth // 8, 4 * width)


def spread_cells(gradient, width):
    coarse_rows = gradient.shape[0]
    coarse_columns = gradient.shape[1]
    shaped = jnp.transpose(
        gradient.reshape(coarse_rows, coarse_columns, 2, 2, width), (0, 2, 1, 3, 4)
    )
    expanded = jnp.broadcast_to(
        shaped[:, :, None, :, :, None, :] / 16.0, (coarse_rows, 2, 4, coarse_columns, 2, 4, width)
    )
    return expanded.reshape(coarse_rows * 8, coarse_columns * 8, width)


def window_mask(block, columns, first_row, first_column, height, breadth):
    query_row = first_row + jnp.arange(block, dtype=jnp.int32)
    query_column = first_column + jnp.arange(columns, dtype=jnp.int32)
    key_row = first_row - 3 + jnp.arange(block + 6, dtype=jnp.int32)
    key_column = first_column - 3 + jnp.arange(columns + 6, dtype=jnp.int32)
    near_row = (
        (jnp.abs(query_row[:, None] - key_row[None, :]) <= 3)
        & (key_row >= 0)[None, :]
        & (key_row < height)[None, :]
    )
    near_column = (
        (jnp.abs(query_column[:, None] - key_column[None, :]) <= 3)
        & (key_column >= 0)[None, :]
        & (key_column < breadth)[None, :]
    )
    joined = near_row[:, None, :, None] & near_column[None, :, None, :]
    return joined.reshape(block * columns, (block + 6) * (columns + 6))


def tile_strip(strip, columns):
    trailing_dims = strip.shape[1:]
    shaped = strip.reshape((8, columns // 8, 8) + trailing_dims)
    return jnp.moveaxis(shaped, 1, 0).reshape((columns // 8, 64) + trailing_dims)


def untile_strip(tiled, columns):
    trailing_dims = tiled.shape[2:]
    shaped = tiled.reshape((columns // 8, 8, 8) + trailing_dims)
    return jnp.moveaxis(shaped, 0, 1).reshape((8 * columns,) + trailing_dims)


def window_tiles(strip, columns):
    channels = strip.shape[2]
    tile_count = columns // 8
    leading = strip[:, :columns].reshape(14, tile_count, 8, channels)
    trailing = jnp.pad(strip[:, 8:], ((0, 0), (0, 2), (0, 0))).reshape(14, tile_count, 8, channels)[
        :, :, :6
    ]
    joined = jnp.concatenate([leading, trailing], axis=2)
    return jnp.transpose(joined, (1, 0, 2, 3)).reshape(tile_count, 196, channels)


def fold_tiles(parts, columns):
    tile_count = parts.shape[0]
    channels = parts.shape[2]
    shaped = jnp.transpose(parts.reshape(tile_count, 14, 14, channels), (1, 0, 2, 3))
    leading = jnp.pad(shaped[:, :, :8].reshape(14, columns, channels), ((0, 0), (0, 6), (0, 0)))
    trailing = jnp.pad(shaped[:, :, 8:], ((0, 0), (0, 0), (0, 2), (0, 0))).reshape(
        14, columns, channels
    )
    trailing = jnp.pad(trailing, ((0, 0), (8, 0), (0, 0)))[:, : columns + 6]
    return leading + trailing


def body(tokens, fine_proj, fine_scale, coarse_proj, coarse_scale, coarse_cot):
    rows, columns, width = tokens.shape
    heads = fine_scale.shape[0]
    depth = width // heads
    count = rows * columns
    tile_count = columns // 8
    row_index = lax.axis_index("row")
    col_index = lax.axis_index("col")
    col_count = lax.axis_size("col")
    height = rows * lax.axis_size("row")
    breadth = columns * col_count
    flat = tokens.reshape(count, width)
    ones_fine = jnp.ones((heads,), jnp.float32)
    mixed = jnp.dot(flat, fine_proj, preferred_element_type=jnp.float32)
    raw_query = mixed[:, :width].reshape(count, heads, depth)
    raw_key = mixed[:, width : 2 * width].reshape(count, heads, depth)
    key_flat = unit_rows(raw_key, ones_fine).astype(jnp.bfloat16).reshape(count, width)
    value_flat = mixed[:, 2 * width :].astype(jnp.bfloat16)
    pairs = jnp.concatenate([key_flat, value_flat], axis=1).reshape(rows, columns, 2 * width)
    padded = padded_2(pairs, (("row", 0), ("col", 1)), 3)
    query_half = unit_rows(raw_query, fine_scale).astype(jnp.bfloat16)

    def strip_masks(first):
        starts = col_index * columns + 8 * jnp.arange(tile_count, dtype=jnp.int32)

        def single(start_column):
            return window_mask(8, 8, row_index * rows + first, start_column, height, breadth)

        return jax.vmap(single)(starts)

    def fine_scores(first):
        near = window_tiles(padded, columns)
        key_block = near[..., :width].reshape(tile_count, 196, heads, depth)
        value_block = near[..., width:].reshape(tile_count, 196, heads, depth)
        query_block = tile_strip(query_half, columns)
        mask = strip_masks(first)
        scores = jnp.einsum(
            "tqhd,tkhd->thqk", query_block, key_block, preferred_element_type=jnp.float32
        )
        weights = jnp.where(mask[:, None], jnp.exp(scores), 0.0)
        return (key_block, value_block, query_block, weights)

    first = 0
    key_block, value_block, query_block, weights = fine_scores(first)
    total = jnp.sum(weights, axis=3)
    summed = jnp.einsum(
        "thqk,tkhd->tqhd",
        weights.astype(jnp.bfloat16),
        value_block,
        preferred_element_type=jnp.float32,
    )
    out_tiles = summed / jnp.transpose(total, (0, 2, 1))[..., None]
    outputs = [out_tiles]
    totals = [total]
    attend_rows = untile_strip(out_tiles, columns)
    resid = flat.astype(jnp.float32) + attend_rows.reshape(count, width)
    merged_grid = merge_cells(resid.reshape(rows, columns, width))
    coarse_rows, coarse_columns, coarse_width = merged_grid.shape
    merged_count = coarse_rows * coarse_columns
    merged = merged_grid.reshape(merged_count, coarse_width)
    normed_half = rms_norm(merged).astype(jnp.bfloat16)
    cheads = coarse_scale.shape[0]
    own_width = coarse_proj.shape[2]
    cdepth = own_width // cheads
    piece = lax.all_gather(normed_half, "col", axis=0, tiled=True)
    own_columns = lax.dynamic_slice_in_dim(piece, col_index * own_width, own_width, 1).astype(
        jnp.float32
    )
    made = jnp.einsum("td,sde->tse", piece, coarse_proj, preferred_element_type=jnp.float32)
    gathered = jnp.concatenate([own_columns[:, None, :], made], axis=1)
    group_rows = gathered.shape[0]
    ones_coarse = jnp.ones((cheads,), jnp.float32)
    raw_cquery = gathered[:, 1].reshape(group_rows, cheads, cdepth)
    raw_ckey = gathered[:, 2].reshape(group_rows, cheads, cdepth)
    coarse_query = unit_rows(raw_cquery, coarse_scale).astype(jnp.bfloat16)
    coarse_key = (
        unit_rows(raw_ckey, ones_coarse).astype(jnp.bfloat16).reshape(group_rows, own_width)
    )
    coarse_value = gathered[:, 3].astype(jnp.bfloat16)
    piece = (
        lax.all_gather(coarse_key, "row", axis=0, tiled=True),
        lax.all_gather(coarse_value, "row", axis=0, tiled=True),
    )
    key_piece = piece[0].reshape(-1, cheads, cdepth)
    value_piece = piece[1].reshape(-1, cheads, cdepth)
    scores = jnp.einsum("qhd,khd->hqk", coarse_query, key_piece, preferred_element_type=jnp.float32)
    add_weights = jnp.exp(scores)
    update = jnp.einsum(
        "hqk,khd->qhd",
        add_weights.astype(jnp.bfloat16),
        value_piece,
        preferred_element_type=jnp.float32,
    )
    total = jnp.sum(add_weights, axis=2)
    coarse_att = update / total.T[:, :, None]
    final = gathered[:, 0] + coarse_att.reshape(group_rows, own_width)
    coarse_out = jnp.transpose(
        final.reshape(col_count, coarse_rows, coarse_columns, own_width), (1, 0, 2, 3)
    ).reshape(coarse_rows, col_count * coarse_columns, own_width)
    cotangent = jnp.transpose(
        coarse_cot.reshape(coarse_rows, col_count, coarse_columns, own_width), (1, 0, 2, 3)
    ).reshape(group_rows, own_width)
    cot_heads = cotangent.reshape(group_rows, cheads, cdepth)
    coarse_delta = jnp.sum(cot_heads.astype(jnp.float32) * coarse_att, axis=2)
    total_rows = total.T
    coarse_own_keys = coarse_key.reshape(group_rows, cheads, cdepth)
    coarse_own_values = coarse_value.reshape(group_rows, cheads, cdepth)
    query_flat = coarse_query.reshape(group_rows, own_width)
    piece = (
        lax.all_gather(coarse_key, "row", axis=0, tiled=True),
        lax.all_gather(coarse_value, "row", axis=0, tiled=True),
    )
    key_piece = piece[0].reshape(-1, cheads, cdepth)
    value_piece = piece[1].reshape(-1, cheads, cdepth)
    scores = jnp.einsum("qhd,khd->hqk", coarse_query, key_piece, preferred_element_type=jnp.float32)
    query_shares = jnp.exp(scores) / total[:, :, None]
    query_share_grad = jnp.einsum(
        "qhd,khd->hqk", cot_heads, value_piece, preferred_element_type=jnp.float32
    )
    query_score_grad = (query_shares * (query_share_grad - coarse_delta.T[:, :, None])).astype(
        jnp.bfloat16
    )
    grad_cq = jnp.einsum(
        "hqk,khd->qhd", query_score_grad, key_piece, preferred_element_type=jnp.float32
    )
    piece = (
        lax.all_gather(query_flat, "row", axis=0, tiled=True),
        lax.all_gather(cotangent, "row", axis=0, tiled=True),
        lax.all_gather(total_rows.astype(jnp.bfloat16), "row", axis=0, tiled=True).astype(
            jnp.float32
        ),
        lax.all_gather(coarse_delta.astype(jnp.bfloat16), "row", axis=0, tiled=True).astype(
            jnp.float32
        ),
    )
    query_piece = piece[0].reshape(-1, cheads, cdepth)
    cot_piece = piece[1].reshape(-1, cheads, cdepth)
    total_piece = piece[2]
    delta_piece = piece[3]
    scores = jnp.einsum(
        "khd,qhd->hkq", coarse_own_keys, query_piece, preferred_element_type=jnp.float32
    )
    key_shares = jnp.exp(scores) / total_piece.T[:, None, :]
    key_share_grad = jnp.einsum(
        "khd,qhd->hkq", coarse_own_values, cot_piece, preferred_element_type=jnp.float32
    )
    key_score_grad = (key_shares * (key_share_grad - delta_piece.T[:, None, :])).astype(
        jnp.bfloat16
    )
    key_sum = jnp.einsum(
        "hkq,qhd->khd", key_score_grad, query_piece, preferred_element_type=jnp.float32
    )
    value_sum = jnp.einsum(
        "hkq,qhd->khd",
        key_shares.astype(jnp.bfloat16),
        cot_piece,
        preferred_element_type=jnp.float32,
    )
    _, pull_cquery = jax.vjp(partial(unit_rows, scales=coarse_scale), raw_cquery)
    _, pull_ckey = jax.vjp(partial(unit_rows, scales=ones_coarse), raw_ckey)
    (raw_cq_grad,) = pull_cquery(grad_cq)
    (raw_ck_grad,) = pull_ckey(key_sum)
    grads_half = jnp.stack(
        [
            raw_cq_grad.reshape(group_rows, own_width),
            raw_ck_grad.reshape(group_rows, own_width),
            value_sum.reshape(group_rows, own_width),
        ],
        axis=1,
    ).astype(jnp.bfloat16)
    cot_float = cotangent.astype(jnp.float32)
    column_start = col_index * own_width
    term = jnp.einsum("tse,sde->td", grads_half, coarse_proj, preferred_element_type=jnp.float32)
    own_part = lax.dynamic_slice_in_dim(term, column_start, own_width, 1) + cot_float
    grad_normed = lax.psum_scatter(
        lax.dynamic_update_slice(term, own_part, (jnp.zeros((), jnp.int32), column_start)).astype(
            jnp.bfloat16
        ),
        "col",
        scatter_dimension=0,
        tiled=True,
    ).astype(jnp.float32)
    _, pull_norm = jax.vjp(rms_norm, merged)
    (grad_merged,) = pull_norm(grad_normed)
    grad_fine = spread_cells(
        grad_merged.reshape(coarse_rows, coarse_columns, coarse_width), width
    ).astype(jnp.bfloat16)
    cot_fine = grad_fine.reshape(count, heads, depth)
    back_pad = jnp.zeros((rows + 6, columns + 6, 2 * width), jnp.float32)
    query_grads = []
    for number, first in enumerate(range(0, rows, 8)):
        key_block, value_block, query_block, weights = fine_scores(first)
        total_block = totals[number]
        shares = weights / total_block[..., None]
        cot_block = tile_strip(cot_fine, columns)
        delta_tiles = jnp.sum(cot_block.astype(jnp.float32) * outputs[number], axis=3)
        delta_block = jnp.transpose(delta_tiles, (0, 2, 1))
        share_grad = jnp.einsum(
            "tqhd,tkhd->thqk", cot_block, value_block, preferred_element_type=jnp.float32
        )
        score_grad = (shares * (share_grad - delta_block[..., None])).astype(jnp.bfloat16)
        query_grads.append(
            untile_strip(
                jnp.einsum(
                    "thqk,tkhd->tqhd", score_grad, key_block, preferred_element_type=jnp.float32
                ),
                columns,
            )
        )
        key_part = jnp.einsum(
            "thqk,tqhd->tkhd", score_grad, query_block, preferred_element_type=jnp.float32
        ).reshape(tile_count, 196, width)
        value_part = jnp.einsum(
            "thqk,tqhd->tkhd",
            shares.astype(jnp.bfloat16),
            cot_block,
            preferred_element_type=jnp.float32,
        ).reshape(tile_count, 196, width)
        back_pad = back_pad.at[first : first + 14].add(
            fold_tiles(jnp.concatenate([key_part, value_part], axis=2), columns)
        )
    from_right = shifted(back_pad[:, :3].astype(jnp.bfloat16), "col", -1).astype(jnp.float32)
    from_left = shifted(back_pad[:, columns + 3 :].astype(jnp.bfloat16), "col", 1).astype(
        jnp.float32
    )
    inner = back_pad[:, 3 : columns + 3]
    inner = inner.at[:, columns - 3 :].add(from_right).at[:, :3].add(from_left)
    from_below = shifted(inner[:3].astype(jnp.bfloat16), "row", -1).astype(jnp.float32)
    from_above = shifted(inner[rows + 3 :].astype(jnp.bfloat16), "row", 1).astype(jnp.float32)
    core = inner[3 : rows + 3].at[rows - 3 :].add(from_below).at[:3].add(from_above)
    core = core.reshape(count, 2 * width)
    _, pull_query = jax.vjp(partial(unit_rows, scales=fine_scale), raw_query)
    _, pull_key = jax.vjp(partial(unit_rows, scales=ones_fine), raw_key)
    (raw_q_grad,) = pull_query(query_grads[0])
    (raw_k_grad,) = pull_key(core[:, :width].reshape(count, heads, depth))
    fine_half = jnp.concatenate(
        [raw_q_grad.reshape(count, width), raw_k_grad.reshape(count, width), core[:, width:]],
        axis=1,
    ).astype(jnp.bfloat16)
    back = lax.dot_general(
        fine_half, fine_proj, (((1,), (1,)), ((), ())), preferred_element_type=jnp.float32
    )
    fine_grad = (
        (grad_fine.reshape(count, width).astype(jnp.float32) + back)
        .astype(jnp.bfloat16)
        .reshape(rows, columns, width)
    )
    return (coarse_out, fine_grad)


def solution(mesh):
    return jax.shard_map(
        body,
        mesh=mesh,
        in_specs=(
            P("row", "col", None),
            P(),
            P(),
            P(None, None, "col"),
            P("col"),
            P("row", None, "col"),
        ),
        out_specs=(P("row", None, "col"), P("row", "col", None)),
        check_vma=False,
    )
```

profile of v0, /device:TPU:1, one launch (start us, length us, event | category | flops | bytes accessed | tf_op | source)
XLA Modules:
  0.0 548.6 jit_solution(17000290949105703262)
XLA Ops:
  7.2 1.4 fusion.102
  9.6 5.5 %collective-permute-start = (bf16[3,32,512]{2,1,0:T(8,128)(2,1)S(1)}, bf16[3,32,512]{2,1,0:T(8,128)(2,1)S(1)}, u32[]{:S(2)}, u32[]{:S(2)}) collective-permute-start(bf16[3,32,512]{2,1,0:T(8,128)(2,1)S(1)} %bitcast.237), channel_id=1, source_target_pairs={{0,16},{16,32},{32,48},{48,64},{64,80},{80,96},{96,112},{112,128},... | collective-permute-start | bytes 294920 | tf_op jit(solution)/shard_map/ppermute | solution.py:19
  15.2 4.7 collective-permute-start.1
  22.3 2.0 collective-permute-start.2
  24.3 1.3 collective-permute-start.3
  25.6 40.0 %all-gather.4 = bf16[1,2048,64]{2,1,0:T(8,128)(2,1)S(1)} all-gather(bf16[1,64,64]{2,1,0:T(8,128)(2,1)S(1)} %copy-done.21), channel_id=6, replica_groups=mesh['row'=32,'col'=16] {'row'}, dimensions={1}, use_global_device_ids=true | all-gather | bytes 270336 | tf_op jit(solution)/shard_map/all_gather | solution.py:243
  69.1 1.3 dynamic-slice.37
  71.0 1.3 dynamic-slice.39
  75.1 1.3 copy.123
  76.3 1.1 copy.119
  80.2 2.2 copy.125
  82.4 2.1 reshape_reshape.4
  84.5 1.1 add_reduce_fusion
  85.9 38.1 %all-gather.6 = bf16[16,4,1024]{2,1,0:T(4,128)(2,1)S(1)} all-gather(bf16[1,4,1024]{2,1,0:T(4,128)(2,1)S(1)} %fusion.79), channel_id=1, replica_groups=mesh['row'=32,'col'=16] {'col'}, dimensions={0}, use_global_device_ids=true | all-gather | bytes 139264 | tf_op jit(solution)/shard_map/all_gather | solution.py:180
  125.7 43.3 %all-gather.1 = bf16[2048,1,64]{2,1,0:T(2,128)(2,1)} all-gather(bf16[64,1,64]{2,1,0:T(2,128)(2,1)S(1)} %copy.129), channel_id=3, replica_groups=mesh['row'=32,'col'=16] {'row'}, dimensions={0}, use_global_device_ids=true | all-gather | bytes 270336 | tf_op jit(solution)/shard_map/all_gather | solution.py:196
  168.9 3.4 copy.130
  173.1 1.9 fusion.95
  174.9 1.4 copy.127
  176.4 37.9 %all-gather = bf16[2048,1,64]{2,1,0:T(2,128)(2,1)} all-gather(bf16[64,1,64]{2,1,0:T(2,128)(2,1)} %copy.127), channel_id=2, replica_groups=mesh['row'=32,'col'=16] {'row'}, dimensions={0}, use_global_device_ids=true | all-gather | bytes 270336 | tf_op jit(solution)/shard_map/all_gather | solution.py:197
  214.3 3.5 copy.128
  218.3 1.9 fusion.66
  222.0 1.4 dynamic-update-slice.15
  224.0 1.4 dynamic-update-slice.14
  225.4 54.1 %all-reduce.7 = (bf16[2048]{0:T(1024)(128)(2,1)}, bf16[2048]{0:T(1024)(128)(2,1)}) all-reduce(bf16[2048]{0:T(1024)(128)(2,1)} %dynamic-update-slice.14, bf16[2048]{0:T(1024)(128)(2,1)} %dynamic-update-slice.15), channel_id=5, replica_groups=mesh['row'=32,'col'=16] {'row'}, use_global_device_ids=true, to_apply=%add.4 | all-reduce | flops 4096 | bytes 16384
  279.5 1.3 div.128
  280.8 37.3 %all-gather.2 = bf16[2048,1,64]{2,1,0:T(2,128)(2,1)} all-gather(bf16[64,1,64]{2,1,0:T(2,128)(2,1)} %copy.132), channel_id=4, replica_groups=mesh['row'=32,'col'=16] {'row'}, dimensions={0}, use_global_device_ids=true | all-gather | bytes 270336 | tf_op jit(solution)/shard_map/all_gather | solution.py:242
  318.1 3.4 copy.133
  321.5 1.3 sub.107
  322.8 1.2 fusion.3
  325.1 2.3 fusion.13
  327.4 1.5 multiply_reduce_fusion.4
  331.2 151.8 %all-reduce.10.cloned.1.call-done = bf16[64,1024]{1,0:T(8,128)(2,1)} async-done(((bf16[64,1024]{1,0:T(8,128)(2,1)}), bf16[64,1024]{1,0:T(8,128)(2,1)}) %all-reduce.10.cloned.1.call-update) | async-done | bytes 131088
  485.6 2.7 convolution_bitcast_fusion
  488.4 1.1 copy.139
  489.7 1.8 fusion.8
  492.3 1.5 convolution_bitcast_fusion.1
  493.8 2.0 copy.147
  495.8 1.9 concatenate.54
  497.8 2.0 copy.149
  499.8 1.9 concatenate.55
  501.8 1.8 maximum_bitcast_fusion
  503.6 1.4 copy-done.7
  507.5 1.3 fusion.89
  508.8 1.4 collective-permute-start.4
  510.3 4.0 collective-permute-start.5
  514.9 1.4 slice.257
  518.8 13.4 %collective-permute-start.6 = (bf16[3,32,512]{2,1,0:T(8,128)(2,1)}, bf16[3,32,512]{2,1,0:T(8,128)(2,1)}, u32[]{:S(2)}, u32[]{:S(2)}) collective-permute-start(bf16[3,32,512]{2,1,0:T(8,128)(2,1)} %get-tuple-element.87), channel_id=1, source_target_pairs={{16,0},{32,16},{48,32},{64,48},{80,64},{96,80},{112,96},{128,112},... | collective-permute-start | bytes 294920 | tf_op jit(solution)/shard_map/ppermute | solution.py:31
  534.7 3.2 collective-permute-start.7
  (227 shorter events, 34.9 us)
Async XLA Ops:
  7.2 117.0 %copy-start = (bf16[3,1024,64]{1,2,0:T(8,128)(2,1)S(1)}, bf16[3,1024,64]{1,2,0:T(8,128)(2,1)}, u32[]{:S(2)}) copy-start(bf16[3,1024,64]{1,2,0:T(8,128)(2,1)} %param.21) | copy-start | bytes 1179652
  7.2 475.8 %all-reduce.10.cloned.1.call-start = ((), (), s32[]{:S(2)}) async-start(), calls=%async_computation | async-start | bytes 262144
  9.5 12.4 %copy-start.4 = (f32[256,256]{1,0:T(8,128)}, f32[256,256]{1,0:T(8,128)S(1)}, u32[]{:S(2)}) copy-start(f32[256,256]{1,0:T(8,128)S(1)} %copy.117) | copy-start | bytes 786436
  9.6 16.0 %copy-start.21 = (bf16[1,64,64]{2,1,0:T(8,128)(2,1)S(1)}, bf16[1,64,64]{2,1,0:T(8,128)(2,1)}, u32[]{:S(2)}) copy-start(bf16[1,64,64]{2,1,0:T(8,128)(2,1)} %param.23) | copy-start | bytes 24580
  9.6 12.5 %collective-permute-start = (bf16[3,32,512]{2,1,0:T(8,128)(2,1)S(1)}, bf16[3,32,512]{2,1,0:T(8,128)(2,1)S(1)}, u32[]{:S(2)}, u32[]{:S(2)}) collective-permute-start(bf16[3,32,512]{2,1,0:T(8,128)(2,1)S(1)} %bitcast.237), channel_id=1, source_target_pairs={{0,16},{16,32},{32,48},{48,64},{64,80},{80,96},{96,112},{112,128},... | collective-permute-start | bytes 294920 | tf_op jit(solution)/shard_map/ppermute | solution.py:19
  15.2 7.0 %collective-permute-start.1 = (bf16[3,32,512]{2,1,0:T(8,128)(2,1)S(1)}, bf16[3,32,512]{2,1,0:T(8,128)(2,1)S(1)}, u32[]{:S(2)}, u32[]{:S(2)}) collective-permute-start(bf16[3,32,512]{2,1,0:T(8,128)(2,1)S(1)} %bitcast.236), channel_id=1, source_target_pairs={{16,0},{32,16},{48,32},{64,48},{80,64},{96,80},{112,96},{128,112},... | collective-permute-start | bytes 294920 | tf_op jit(solution)/shard_map/ppermute | solution.py:21
  21.4 44.4 %copy-start.17 = (bf16[8,32,256]{2,1,0:T(8,128)(2,1)S(1)}, bf16[8,32,256]{2,1,0:T(8,128)(2,1)}, u32[]{:S(2)}) copy-start(bf16[8,32,256]{2,1,0:T(8,128)(2,1)} %param.18) | copy-start | bytes 393220
  22.0 3.6 copy-start.2
  22.1 2.2 copy-start.28
  22.2 46.2 %copy-start.33 = (f32[4]{0:T(128)S(1)}, f32[4]{0:T(128)}, u32[]{:S(2)}) copy-start(f32[4]{0:T(128)} %param.20) | copy-start | bytes 52
  22.3 50.7 %collective-permute-start.2 = (bf16[14,3,512]{2,1,0:T(4,128)(2,1)S(1)}, bf16[14,3,512]{2,1,0:T(4,128)(2,1)S(1)}, u32[]{:S(2)}, u32[]{:S(2)}) collective-permute-start(bf16[14,3,512]{2,1,0:T(4,128)(2,1)S(1)} %get-tuple-element.90), channel_id=1, source_target_pairs={{0,1},{1,2},{2,3},{3,4},{4,5},{5,6},{6,7},{7,8},{8,9},{9,10},{10,1... | collective-permute-start | bytes 129032 | tf_op jit(solution)/shard_map/ppermute | solution.py:19
  24.3 48.6 %collective-permute-start.3 = (bf16[14,3,512]{2,1,0:T(4,128)(2,1)S(1)}, bf16[14,3,512]{2,1,0:T(4,128)(2,1)S(1)}, u32[]{:S(2)}, u32[]{:S(2)}) collective-permute-start(bf16[14,3,512]{2,1,0:T(4,128)(2,1)S(1)} %get-tuple-element.91), channel_id=1, source_target_pairs={{1,0},{2,1},{3,2},{4,3},{5,4},{6,5},{7,6},{8,7},{9,8},{10,9},{11,1... | collective-permute-start | bytes 129032 | tf_op jit(solution)/shard_map/ppermute | solution.py:21
  66.8 10.6 %copy-start.15 = (f32[8,4,8,4]{2,0,3,1:T(8,128)}, f32[8,4,8,4]{2,0,3,1:T(8,128)S(1)}, u32[]{:S(2)}) copy-start(f32[8,4,8,4]{2,0,3,1:T(8,128)S(1)} %copy.121) | copy-start | bytes 12292
  77.4 1.5 copy-start.18
  77.9 2.3 copy-start.30
  79.2 6.5 %copy-start.9 = (f32[4,64,4,64]{1,3,2,0:T(8,128)}, f32[4,64,4,64]{1,3,2,0:T(8,128)S(1)}, u32[]{:S(2)}) copy-start(f32[4,64,4,64]{1,3,2,0:T(8,128)S(1)} %fusion.9) | copy-start | bytes 786436
  85.8 38.3 %copy-start.48 = (f32[4]{0:T(128)}, f32[4]{0:T(128)S(1)}, u32[]{:S(2)}) copy-start(f32[4]{0:T(128)S(1)} %multiply_reduce_fusion.7) | copy-start | bytes 52
  85.8 39.2 %copy-start.36 = (f32[4]{0:T(128)}, f32[4]{0:T(128)S(1)}, u32[]{:S(2)}) copy-start(f32[4]{0:T(128)S(1)} %fusion.84) | copy-start | bytes 52
  125.6 46.8 %copy-start.24 = (bf16[64,1,64]{0,2,1:T(8,128)(2,1)}, bf16[64,1,64]{0,2,1:T(8,128)(2,1)S(1)}, u32[]{:S(2)}) copy-start(bf16[64,1,64]{0,2,1:T(8,128)(2,1)S(1)} %get-tuple-element.97) | copy-start | bytes 24580
  174.9 42.8 %copy-start.42 = (f32[64]{0:T(128)S(1)}, f32[64]{0:T(128)}, u32[]{:S(2)}) copy-start(f32[64]{0:T(128)} %get-tuple-element.102) | copy-start | bytes 772
  218.3 104.5 %copy-start.25 = (bf16[64,1,64]{0,2,1:T(8,128)(2,1)S(1)}, bf16[64,1,64]{0,2,1:T(8,128)(2,1)}, u32[]{:S(2)}) copy-start(bf16[64,1,64]{0,2,1:T(8,128)(2,1)} %copy-done.24) | copy-start | bytes 24580
  327.4 1.5 copy-start.46
  327.4 1.6 copy-start.44
  327.4 1.6 copy-start.23
  327.4 1.6 copy-start.39
  327.4 1.6 copy-start.41
  327.4 3.1 copy-start.22
  327.4 156.4 %copy-start.49 = (f32[4]{0:T(128)S(1)}, f32[4]{0:T(128)}, u32[]{:S(2)}) copy-start(f32[4]{0:T(128)} %copy-done.48) | copy-start | bytes 52
  327.4 156.4 %copy-start.37 = (f32[4]{0:T(128)S(1)}, f32[4]{0:T(128)}, u32[]{:S(2)}) copy-start(f32[4]{0:T(128)} %copy-done.36) | copy-start | bytes 52
  328.9 156.7 %copy-start.31 = (f32[4,4,64]{2,1,0:T(4,128)S(1)}, f32[4,4,64]{2,1,0:T(4,128)}, u32[]{:S(2)}) copy-start(f32[4,4,64]{2,1,0:T(4,128)} %copy-done.30) | copy-start | bytes 12292
  485.6 3.9 copy-start.10
  485.6 4.0 copy-start.32
  489.6 2.6 copy-start.16
  489.6 2.6 copy-start.34
  503.5 2.5 copy-start.1
  503.5 1.4 copy-start.7
  506.1 1.2 slice-start
  507.5 6.7 %copy-start.8 = (f32[4,64,4,64]{1,3,2,0:T(8,128)S(1)}, f32[4,64,4,64]{1,3,2,0:T(8,128)}, u32[]{:S(2)}) copy-start(f32[4,64,4,64]{1,3,2,0:T(8,128)} %convolution_bitcast_fusion.2) | copy-start | bytes 786436
  508.8 5.9 %copy-start.3 = (f32[256,256]{0,1:T(8,128)S(1)}, f32[256,256]{0,1:T(8,128)}, u32[]{:S(2)}) copy-start(f32[256,256]{0,1:T(8,128)} %copy-done.2) | copy-start | bytes 786436
  508.8 7.4 %collective-permute-start.4 = (bf16[14,3,512]{2,1,0:T(4,128)(2,1)S(1)}, bf16[14,3,512]{2,1,0:T(4,128)(2,1)S(1)}, u32[]{:S(2)}, u32[]{:S(2)}) collective-permute-start(bf16[14,3,512]{2,1,0:T(4,128)(2,1)S(1)} %get-tuple-element.85), channel_id=1, source_target_pairs={{1,0},{2,1},{3,2},{4,3},{5,4},{6,5},{7,6},{8,7},{9,8},{10,9},{11,1... | collective-permute-start | bytes 129032 | tf_op jit(solution)/shard_map/ppermute | solution.py:31
  510.3 7.3 %collective-permute-start.5 = (bf16[14,3,512]{2,1,0:T(4,128)(2,1)S(1)}, bf16[14,3,512]{2,1,0:T(4,128)(2,1)S(1)}, u32[]{:S(2)}, u32[]{:S(2)}) collective-permute-start(bf16[14,3,512]{2,1,0:T(4,128)(2,1)S(1)} %get-tuple-element.84), channel_id=1, source_target_pairs={{0,1},{1,2},{2,3},{3,4},{4,5},{5,6},{6,7},{7,8},{8,9},{9,10},{10,1... | collective-permute-start | bytes 129032 | tf_op jit(solution)/shard_map/ppermute | solution.py:31
  516.3 15.9 %copy-start.29 = (f32[256,4]{0,1:T(4,128)S(1)}, f32[256,4]{0,1:T(4,128)}, u32[]{:S(2)}) copy-start(f32[256,4]{0,1:T(4,128)} %copy-done.28) | copy-start | bytes 12292
  518.8 19.1 %collective-permute-start.6 = (bf16[3,32,512]{2,1,0:T(8,128)(2,1)}, bf16[3,32,512]{2,1,0:T(8,128)(2,1)}, u32[]{:S(2)}, u32[]{:S(2)}) collective-permute-start(bf16[3,32,512]{2,1,0:T(8,128)(2,1)} %get-tuple-element.87), channel_id=1, source_target_pairs={{16,0},{32,16},{48,32},{64,48},{80,64},{96,80},{112,96},{128,112},... | collective-permute-start | bytes 294920 | tf_op jit(solution)/shard_map/ppermute | solution.py:31
  533.8 5.8 %copy-start.13 = (f32[256,256]{1,0:T(8,128)S(1)}, f32[256,256]{1,0:T(8,128)}, u32[]{:S(2)}) copy-start(f32[256,256]{1,0:T(8,128)} %copy.142) | copy-start | bytes 786436
  533.8 5.8 %copy-start.14 = (f32[256,256]{1,0:T(8,128)S(1)}, f32[256,256]{1,0:T(8,128)}, u32[]{:S(2)}) copy-start(f32[256,256]{1,0:T(8,128)} %copy.145) | copy-start | bytes 786436
  533.8 5.8 %copy-start.35 = (f32[256]{0:T(256)S(1)}, f32[256]{0:T(256)}, u32[]{:S(2)}) copy-start(f32[256]{0:T(256)} %mul.349) | copy-start | bytes 3076
  534.7 4.8 collective-permute-start.7
  539.7 1.1 copy-start.20
  (12 other events, 8.7 us)
Sparse Core Ops, SparseCore 0:
  330.6 152.3 all-reduce.9
where the time goes:
time: 558 us; the launch traced here: 549 us
  blocking collectives  251 us (45%)
  waiting for transfers between devices  153 us (27%)
  local copies, waits for them, and re-layouts  58.1 us (10%)
  starting transfers between devices  35.5 us (6%)
  matrix products  19.7 us (4%)
  between operations  17.2 us (3%)
  other arithmetic  14.8 us (3%)
    unnamed x2, waiting for transfers between devices  152 us
    unnamed x1, blocking collectives  54.1 us
    all_gather x1, blocking collectives, body(): lax.all_gather(coarse_key, 'row', axis=0, tiled=True)  43.3 us
    all_gather x1, blocking collectives, body(): lax.all_gather(cotangent, 'row', axis=0, tiled=True)  40 us
    all_gather x1, blocking collectives, body(): piece = lax.all_gather(normed_half, 'col', axis=0, tiled=True)  38.1 us
    all_gather x1, blocking collectives, body(): lax.all_gather(coarse_value, 'row', axis=0, tiled=True)  37.9 us
    all_gather x1, blocking collectives, body(): lax.all_gather(query_flat, 'row', axis=0, tiled=True)  37.3 us
    ppermute x4, starting transfers between devices, shifted(): lax.ppermute(value, axis, [(source, source + steps) for source in range(f...  22 us
  transfers between devices with their start and end apart: 9, of which 2 were waited for; matrix products, arithmetic and copies ran while one was open for 3% of the time, Pallas kernels for 0%

commit v1 on v0

v1 whole, which is shorter than its diff:
```python
import contextlib

import jax
import jax.numpy as jnp
from jax import lax
from jax.experimental import pallas as pl
from jax.experimental.pallas import tpu as pltpu
from jax.sharding import PartitionSpec as P

F32 = jnp.float32
BF = jnp.bfloat16
I32 = jnp.int32
EPS = 1e-06
MESH = pl.DeviceIdType.MESH

NY, NZ, NCORE = 2, 8, 2
NR, NC = NY * NZ * NCORE, 16
ROWS, COLS, WIDTH, HEADS = 8, 32, 256, 4
TOKENS = ROWS * COLS
HALO = 320
KEYS = 640
OWN = slice(0, 256)
HALF_HALO = (slice(256, 512), slice(384, 640))
CT = 4 * NC
CD = 64
NM = NY * NCORE

DIRS = ((-1, 0), (1, 0), (0, -1), (0, 1), (-1, -1), (-1, 1), (1, -1), (1, 1))
OPPOSITE = (1, 0, 3, 2, 7, 6, 5, 4)
START = (0, 96, 192, 224, 256, 272, 288, 304)
PLACE = (288, 512, 384, 416, 448, 464, 480, 496)
LENGTH = (96, 96, 32, 32, 16, 16, 16, 16)


def mm(a, b):
    return jnp.dot(a, b, preferred_element_type=F32)


def mt(a, b):
    return lax.dot_general(a, b, (((1,), (1,)), ((), ())), preferred_element_type=F32)


def iota(shape, dim):
    return lax.broadcasted_iota(I32, shape, dim)


def onehot(condition):
    return jnp.where(condition, 1.0, 0.0).astype(BF)


def third(m):
    return (m * 11) >> 5


def edge_parts(p):
    side = p < 64
    m = jnp.where(side, p & 31, p & 15)
    down = third(m)
    across = m - 3 * down
    right = jnp.where(side, (p >> 5) & 1, (p >> 4) & 1)
    bottom = jnp.where(side, 0, ((p - 64) >> 5) & 1)
    used = m < jnp.where(side, 24, 9)
    return side, down, across, right, bottom, used


def kernel(
    tok_hbm, fproj_hbm, fscale_hbm, cproj, cscale, cot_hbm,
    out_c, out_f,
    tok, fproj, fscale, cot, kvx, staging, rq_s, rk_s, iq_s, ik_s, qh, qt, pt, psum, fot, fo_s, kt, fproj_t, wxt, wide, cg, mm_s, inv_s,
    eye_s, w_kv, w_qc, select_s,
    kv, qc, st, ce_s, dp_s, cds_s, dkv, dkv_in, dqo, dqo_in, sb, rb, dyt, ds, dk_halo, dv_halo, rh_k, rh_v,
    in_sem, w_sem, halo_ss, halo_rs, cg_ss, cg_rs, kv_ss, kv_rs, qc_ss, qc_rs, st_ss, st_rs,
    dkv_ss, dkv_rs, dqo_ss, dqo_rs, rs_ss, rs_rs, back_ss, back_rs,
):
    row = lax.axis_index("row")
    col = lax.axis_index("col")
    core = row % NCORE
    z = (row // NCORE) % NZ
    y = row // (NCORE * NZ)
    mate = y * NCORE + core
    col_hi = col // 4
    col_lo = col % 4

    def index_of(m, zz):
        return ((m // NCORE) * NZ + zz) * NCORE + m % NCORE

    def neighbour(k):
        return (row + DIRS[k][0] + NR) % NR, (col + DIRS[k][1] + NC) % NC

    z_steps = (4, 3, 5, 2, 6, 1, 7)
    col_steps = sorted(
        ((hi, lo) for hi in range(4) for lo in range(4) if (hi, lo) != (0, 0)),
        key=lambda s: -(2 * min(s[0], 4 - s[0]) + min(s[1], 4 - s[1])),
    )
    z_peers = [(z + d) % NZ for d in z_steps]
    mates = [(mate + d) % NM for d in range(1, NM)]
    col_peers = [((col_hi + hi) % 4) * 4 + (col_lo + lo) % 4 for hi, lo in col_steps]

    open_scope = contextlib.ExitStack()

    def phase(name):
        open_scope.close()
        open_scope.enter_context(jax.named_scope(name))

    barrier = pltpu.get_barrier_semaphore()

    def greet(r, c):
        pl.semaphore_signal(barrier, inc=1, device_id=(r, c), device_id_type=MESH)

    phase("greet")
    for c in col_peers[0:9]:
        greet(row, c)
    for k in range(4, 8):
        greet(*neighbour(k))
    for zz in z_peers[0:3]:
        greet(index_of(mate, zz), col)

    copies = [
        pltpu.make_async_copy(tok_hbm, tok, in_sem.at[0]),
        pltpu.make_async_copy(fproj_hbm, fproj, in_sem.at[1]),
        pltpu.make_async_copy(cot_hbm, cot, in_sem.at[2]),
        pltpu.make_async_copy(fscale_hbm, fscale, in_sem.at[3]),
    ]
    for c in copies:
        c.start()
    weight_copies = [
        pltpu.make_async_copy(cproj.at[s], wxt.at[pl.ds(i * CD, CD)], w_sem.at[i])
        for i, s in enumerate((1, 2, 0))
    ]
    for c in col_peers[9:]:
        greet(row, c)
    for zz in z_peers[3:]:
        greet(index_of(mate, zz), col)
    greet((row + 2 * core - 1 + NR) % NR, col)
    for m in mates:
        greet(index_of(m, z), col)

    phase("inputs_wait")
    lane = iota((1, WIDTH), 1)
    head_mask = [jnp.where((lane >> 6) == h, 1.0, 0.0) for h in range(HEADS)]
    blocks = onehot((iota((WIDTH, WIDTH), 0) >> 6) == (iota((WIDTH, WIDTH), 1) >> 6))
    for c in copies[0:2]:
        c.wait()
    for c in weight_copies:
        c.start()
    phase("projection")
    token = tok[...]
    raw_k = mm(token, fproj[:, WIDTH : 2 * WIDTH])
    inv_k = lax.rsqrt(mm((raw_k * raw_k).astype(BF), blocks) + EPS)
    unit_k = (raw_k * inv_k).astype(BF)
    value = mm(token, fproj[:, 2 * WIDTH :]).astype(BF)
    kvx[OWN, 0:WIDTH] = unit_k
    kvx[OWN, WIDTH : 2 * WIDTH] = value
    kvx[256:288, :] = jnp.zeros((32, 2 * WIDTH), BF)
    kvx[608:640, :] = jnp.zeros((32, 2 * WIDTH), BF)

    def edge_token(slot):
        side, down, across, right, bottom, used = edge_parts(slot)
        return jnp.where(used, (down + 5 * bottom) * COLS + across + (COLS - 3) * right, -1)

    select = onehot(edge_token(iota((128, TOKENS), 0)) == iota((128, TOKENS), 1))
    staging[:, 0:WIDTH] = mm(select, unit_k).astype(BF)
    staging[:, WIDTH : 2 * WIDTH] = mm(select, value).astype(BF)
    rk_s[...] = raw_k
    ik_s[...] = inv_k

    phase("barrier_wait")
    pl.semaphore_wait(barrier, len(col_peers) + len(z_peers) + len(mates) + 5)

    phase("halo_send")
    def remote(src, dst, ss, rs, r, c):
        return pltpu.make_async_remote_copy(
            src_ref=src, dst_ref=dst, send_sem=ss, recv_sem=rs, device_id=(r, c), device_id_type=MESH
        )

    def halo_copy(k):
        o = OPPOSITE[k]
        if k == 0:
            source = kvx.at[pl.ds(OWN.start, 96)]
        elif k == 1:
            source = kvx.at[pl.ds(OWN.stop - 96, 96)]
        else:
            source = staging.at[pl.ds(START[k] - 192, LENGTH[k])]
        target = kvx.at[pl.ds(PLACE[o], LENGTH[o])]
        return remote(source, target, halo_ss.at[k], halo_rs.at[k], *neighbour(k))

    def start_all(copy):
        for k in (4, 5, 6, 7, 2, 3):
            copy(k).start()

        @pl.when(core == 0)
        def _():
            copy(0).start()
            copy(1).start()

        @pl.when(core == 1)
        def _():
            copy(1).start()
            copy(0).start()

    start_all(halo_copy)

    phase("own_attend")
    for c in copies[2:4]:
        c.wait()
    gain = sum(head_mask[h] * fscale[h] for h in range(HEADS))
    raw_q = mm(token, fproj[:, 0:WIDTH])
    inv_q = lax.rsqrt(mm((raw_q * raw_q).astype(BF), blocks) + EPS)
    unit_q = raw_q * inv_q * gain
    rq_s[...] = raw_q
    iq_s[...] = inv_q

    def head(h, size):
        return slice(h * size, (h + 1) * size)

    half_size = TOKENS // 2
    groups = [(half, pair) for half in range(2) for pair in range(2)]

    def lanes_of(half, pair):
        return head(2 * half + pair, 2 * half_size)

    for half in range(2):
        for h in range(HEADS):
            rows = unit_q[head(half, half_size), :] * head_mask[h]
            qh[head(HEADS * half + h, half_size), :] = rows.astype(BF)
    eye_s[...] = onehot(iota((WIDTH, WIDTH), 0) == iota((WIDTH, WIDTH), 1))

    def transposed(x):
        return mt(eye_s[...], x)

    def spread_heads(ref, x_t):
        for h in range(HEADS):
            rows = head(h, CD)
            for half in range(2):
                lanes = head(HEADS * half + h, half_size)
                ref[rows, lanes] = x_t[rows, head(half, half_size)].astype(BF)

    qt[...] = jnp.zeros((WIDTH, HEADS * TOKENS), BF)
    spread_heads(qt, transposed(unit_q.astype(BF)))

    def near(half, k_row, k_col):
        q = iota((1, 2 * half_size), 1)
        q_row = half * (ROWS // 2) + ((q & (half_size - 1)) >> 5)
        q_col = q & (COLS - 1)
        seen = (jnp.abs(q_row - k_row) <= 3) & (jnp.abs(q_col - k_col) <= 3)
        return jnp.where(seen, 1.0, 0.0)

    def in_image(k_row, k_col, used):
        k_row_all = k_row + row * ROWS
        k_col_all = k_col + col * COLS
        used = used & (k_row_all >= 0) & (k_row_all < ROWS * NR)
        used = used & (k_col_all >= 0) & (k_col_all < COLS * NC)
        return jnp.where(used, k_row, 1000)

    def attend(part, half, values_t, mask):
        keys = kvx[part, 0:WIDTH]
        sums, outs = [], []
        for pair in range(2):
            lanes = lanes_of(half, pair)
            e = jnp.exp(mm(keys, qt[:, lanes])) * mask
            pt[part, lanes] = e
            sums.append(jnp.sum(e, axis=0, keepdims=True))
            outs.append(mm(values_t[head(pair, 2 * CD), :], e.astype(BF)))
        return sums, outs

    values_t = transposed(value).astype(BF)
    n = iota((TOKENS, 1), 0)
    sums = []
    for half in range(2):
        new, outs = attend(OWN, half, values_t, near(half, n >> 5, n & (COLS - 1)))
        sums += new
        for pair in range(2):
            fot[head(2 * half + pair, 2 * CD), :] = outs[pair]

    phase("masks")
    def pooled(r, t):
        return (
            ((r >> 3) == (t >> 7))
            & (((r >> 2) & 1) == ((t >> 2) & 1))
            & ((r & 3) == ((t & 31) >> 3))
        )

    pool = jnp.where(pooled(iota((16, TOKENS), 0), iota((16, TOKENS), 1)), 1.0 / 16.0, 0.0).astype(BF)
    merged_tokens = mm(pool, token)
    n = iota((KEYS - TOKENS, 1), 0)
    side, down, across, right, bottom, used = edge_parts(n - 128)
    k_row = jnp.where(side, down, down - 3 + 11 * bottom)
    k_col = across - 3 + (COLS + 3) * right
    k_row = jnp.where(n < 128, ((n - 32) >> 5) - 3, jnp.where(n < 256, k_row, ((n - 256) >> 5) + ROWS))
    k_col = jnp.where((n >= 128) & (n < 256), k_col, n & (COLS - 1))
    used = (used | (n < 128) | (n >= 256)) & (n >= 32) & (n < 352)
    k_row = in_image(k_row, k_col, used)
    mask_halo = []
    for half in range(2):
        rows = slice(half * 128, half * 128 + 256)
        mask_halo.append(near(half, k_row[rows, :], k_col[rows, :]))

    phase("halo_wait")
    for k in range(8):
        halo_copy(OPPOSITE[k]).wait_recv()

    phase("halo_attend")
    halo_t = transposed(kvx[TOKENS:KEYS, WIDTH : 2 * WIDTH]).astype(BF)
    linv, outs_all = [], []
    for half in range(2):
        halo_values = halo_t[:, half * 128 : half * 128 + 256]
        more_sums, more_outs = attend(HALF_HALO[half], half, halo_values, mask_halo[half])
        for pair in range(2):
            g = 2 * half + pair
            linv.append(1.0 / (sums[g] + more_sums[pair]))
            outs_all.append((fot[head(g, 2 * CD), :] + more_outs[pair]) * linv[g])

    def join_heads(pieces):
        rows = []
        for pair in range(2):
            for h in range(2):
                blocks_of = [
                    pieces[2 * half + pair][head(h, CD), head(h, half_size)] for half in range(2)
                ]
                rows.append(jnp.concatenate(blocks_of, axis=1))
        return jnp.concatenate(rows, axis=0)

    fo_t = join_heads(outs_all).astype(BF)

    phase("merge")
    merged = merged_tokens + mt(pool, fo_t)

    def token_sum(x):
        x = x[0:8, :] + x[8:16, :]
        x = jnp.sum(x + pltpu.roll(x, 4, 0), axis=1, keepdims=True)
        return jnp.concatenate([x, x], axis=0)

    inv_m = lax.rsqrt(token_sum(merged * merged) * (1.0 / (4 * WIDTH)) + EPS)

    def part16(i):
        return pl.ds(pl.multiple_of(i * 16, 16), 16)

    cg[part16(col), :] = (merged * inv_m).astype(BF)

    phase("cn_send")
    for c in col_peers:
        remote(cg.at[part16(col)], cg.at[part16(col)], cg_ss, cg_rs, row, c).start()
    col_bytes = pl.ds(0, 16 * len(col_peers))
    cg_all = remote(cg.at[col_bytes], cg.at[col_bytes], cg_ss, cg_rs, row, col_peers[0])

    phase("cn_beside")
    mm_s[...] = merged
    inv_s[...] = inv_m
    depth = iota((CD, 4 * WIDTH), 1)
    wxt[3 * CD : 4 * CD, :] = onehot(depth == col * CD + iota((CD, 4 * WIDTH), 0))
    shift_up = onehot(iota((CD, 2 * CD), 1) == iota((CD, 2 * CD), 0) + CD)
    cot_high = mm(cot[...], shift_up)
    low_lane = iota((1, 2 * CD), 1) < CD
    for c in weight_copies:
        c.wait()
    for ab in range(4):
        wide[head(ab, WIDTH), :] = mt(eye_s[...], wxt[:, head(ab, WIDTH)]).astype(BF)
    for half, pair in groups:
        lanes = lanes_of(half, pair)
        for part in (OWN, HALF_HALO[half]):
            pt[part, lanes] = pt[part, lanes] * linv[2 * half + pair]
    for k in range(8):
        halo_copy(k).wait_send()
    phase("cn_wait")
    cg_all.wait_recv()

    phase("coarse_projection")
    part_of = (iota((16 * NC, 1), 0) >> 2) & 3
    part_mask = [jnp.where(part_of == ab, 1.0, 0.0) for ab in range(4)]
    upper_rows = iota((1, 8, 1), 1) < 4

    def by_part(x):
        return jnp.concatenate([(x * part_mask[ab]).astype(BF) for ab in range(4)], axis=1)

    made = mm(by_part(cg[...].astype(F32)), wide[...]).reshape(NC, 2, 8, 4 * CD)
    made = made[:, 0] + made[:, 1]
    made = made + pltpu.roll(made, 4, 1)
    made = made.reshape(NC // 2, 2, 8, 4 * CD)
    made = jnp.where(upper_rows, made[:, 0], made[:, 1]).reshape(CT, 4 * CD)
    made_kv = made[:, 0 : 2 * CD]
    made_qo = made[:, 2 * CD : 4 * CD]

    def low_sum(x):
        return jnp.sum(jnp.where(low_lane, x, 0.0), axis=1, keepdims=True)

    coarse_gain = cscale[0]
    inv_ck = lax.rsqrt(low_sum(made_kv * made_kv) + EPS)
    inv_cq = lax.rsqrt(low_sum(made_qo * made_qo) + EPS)
    own_kv = jnp.where(low_lane, made_kv * inv_ck, made_kv)
    own_qc = jnp.where(low_lane, made_qo * inv_cq * coarse_gain, cot_high)

    def block(i):
        return pl.ds(pl.multiple_of(i * CT, CT), CT)

    kv[block(z), :] = own_kv.astype(BF)
    qc[block(mate), :] = own_qc.astype(BF)

    phase("kv_send")
    def kv_copy(slot_of, to, d):
        return remote(
            kv.at[block(slot_of)], kv.at[block(slot_of)], kv_ss, kv_rs.at[d], index_of(mate, to), col
        )

    for d, zz in zip(z_steps, z_peers):
        kv_copy(z, zz, d).start()
    for m in mates:
        remote(qc.at[block(mate)], qc.at[block(mate)], qc_ss, qc_rs, index_of(m, z), col).start()
    z_bytes = pl.ds(0, CT * len(z_peers))
    m_bytes = pl.ds(0, CT * len(mates))
    to_z = (index_of(mate, z_peers[0]), col)
    to_mate = (index_of(mates[0], z), col)
    qc_all = remote(qc.at[m_bytes], qc.at[m_bytes], qc_ss, qc_rs, *to_mate)
    phase("kv_beside")
    cg_all.wait_send()
    for ab in range(4):
        w_kv[head(ab, 2 * CD), :] = wxt[0 : 2 * CD, head(ab, WIDTH)]
        w_qc[head(ab, 2 * CD), :] = wxt[2 * CD : 4 * CD, head(ab, WIDTH)]
    fo_s[...] = fo_t.astype(F32)
    kt[...] = transposed(kvx[:, 0:WIDTH]).astype(BF)
    for i in range(3):
        fproj_t[head(i, WIDTH), :] = transposed(fproj[:, head(i, WIDTH)]).astype(BF)
    phase("qc_wait")
    qc_all.wait_recv()
    queries = qc[...].astype(F32)
    q_low = jnp.where(low_lane, queries, 0.0).astype(BF)
    cot_only = jnp.where(low_lane, 0.0, queries).astype(BF)
    eye_small = eye_s[0 : 2 * CD, 0 : 2 * CD]
    q_low_t = mt(eye_small, q_low).astype(BF)
    cot_t = mt(eye_small, cot_only).astype(BF)

    phase("kv_scores")
    c_sum = jnp.zeros((1, NM * CT), F32)
    c_weighted = jnp.zeros((1, NM * CT), F32)
    for steps in ((0, 1, 7), (2, 6), (3, 5, 4)):
        sources = [(z + NZ - d) % NZ for d in steps]
        for d, source in zip(steps, sources):
            if d:
                kv_copy(source, source, d).wait_recv()
        some = jnp.concatenate([kv[block(source), :] for source in sources], axis=0)
        e = jnp.exp(mm(some, q_low_t))
        p = mm(some, cot_t)
        for i, source in enumerate(sources):
            ce_s[block(source), :] = e[head(i, CT), :]
            dp_s[block(source), :] = p[head(i, CT), :]
        c_sum = c_sum + jnp.sum(e, axis=0, keepdims=True)
        c_weighted = c_weighted + jnp.sum(e * p, axis=0, keepdims=True)
    phase("stats_send")
    st[mate, 0:1, :] = c_sum
    st[mate, 1:2, :] = c_weighted
    for m in mates:
        remote(st.at[mate], st.at[mate], st_ss, st_rs, index_of(m, z), col).start()
    st_bytes = pl.ds(0, len(mates))
    st_all = remote(st.at[st_bytes], st.at[st_bytes], st_ss, st_rs, *to_mate)
    phase("stats_beside")
    kv_t = mt(eye_s[0 : 2 * CD, 0 : 2 * CD], kv[...]).astype(BF)
    o_t = mm(kv_t, ce_s[...].astype(BF))
    remote(kv.at[z_bytes], kv.at[z_bytes], kv_ss, kv_rs.at[1], *to_z).wait_send()
    qc_all.wait_send()
    phase("stats_wait")
    st_all.wait_recv()
    phase("dkv_make")
    totals = (st[0] + st[1]) + (st[2] + st[3])
    c_inv = 1.0 / totals[0:1, :]
    c_delta = totals[1:2, :] * c_inv
    both = jnp.concatenate([q_low, cot_only], axis=0)
    for targets in (z_peers[0:3], z_peers[3:5], z_peers[5:7] + [z]):
        cp = jnp.concatenate([ce_s[block(zz), :] for zz in targets], axis=0) * c_inv
        cds = cp * (jnp.concatenate([dp_s[block(zz), :] for zz in targets], axis=0) - c_delta)
        cds = cds.astype(BF)
        made_here = mm(jnp.concatenate([cds, cp.astype(BF)], axis=1), both).astype(BF)
        for i, zz in enumerate(targets):
            cds_s[block(zz), :] = cds[head(i, CT), :]
            dkv[block(zz), :] = made_here[head(i, CT), :]
            if zz is not z:
                remote(
                    dkv.at[block(zz)], dkv_in.at[block(z)], dkv_ss, dkv_rs, index_of(mate, zz), col
                ).start()
    dkv_all = remote(dkv.at[z_bytes], dkv_in.at[z_bytes], dkv_ss, dkv_rs, *to_z)
    phase("dq_make")
    dq_t = mm(kv_t, cds_s[...])
    dqo_t = jnp.where(iota((2 * CD, 1), 0) < CD, dq_t, o_t * c_inv).astype(BF)
    dqo[...] = transposed(dqo_t).astype(BF)
    for m in mates:
        remote(dqo.at[block(m)], dqo_in.at[block(mate)], dqo_ss, dqo_rs, index_of(m, z), col).start()
    dqo_all = remote(dqo.at[m_bytes], dqo_in.at[m_bytes], dqo_ss, dqo_rs, *to_mate)
    dkv_in[block(z), :] = dkv[block(z), :]
    dqo_in[block(mate), :] = dqo[block(mate), :]
    st_all.wait_send()
    phase("dqo_wait")
    dqo_all.wait_recv()
    phase("dq_unit")
    d_qo = dqo_in[head(0, CT), :].astype(F32)
    for m in range(1, NM):
        d_qo = d_qo + dqo_in[head(m, CT), :].astype(F32)
    g_q = (coarse_gain * inv_cq) * (d_qo - made_qo * (inv_cq * inv_cq * low_sum(d_qo * made_qo)))

    def repeated(g):
        g = g.reshape(NC // 2, 8, 2 * CD)
        turned = pltpu.roll(g, 4, 1)
        pair = [jnp.where(upper_rows, g, turned), jnp.where(upper_rows, turned, g)]
        g = jnp.stack(pair, axis=1).reshape(NC, 1, 8, 2 * CD)
        return jnp.broadcast_to(g, (NC, 2, 8, 2 * CD)).reshape(16 * NC, 2 * CD)

    term_qc = mm(by_part(repeated(jnp.where(low_lane, g_q, cot_high))), w_qc[...])
    phase("dkv_wait")
    dkv_all.wait_recv()
    phase("term")
    d_kv = dkv_in[head(0, CT), :].astype(F32)
    for i in range(1, NZ):
        d_kv = d_kv + dkv_in[head(i, CT), :].astype(F32)
    g_k = inv_ck * (d_kv - made_kv * (inv_ck * inv_ck * low_sum(d_kv * made_kv)))
    g_kv = jnp.where(low_lane, g_k, d_kv)

    sb[...] = (term_qc + mm(by_part(repeated(g_kv)), w_kv[...])).astype(BF)
    phase("rs_send")
    for c in col_peers:
        remote(sb.at[part16(c)], rb.at[part16(col)], rs_ss, rs_rs, row, c).start()
    rs_all = remote(sb.at[col_bytes], rb.at[col_bytes], rs_ss, rs_rs, row, col_peers[0])
    phase("rs_beside")
    rb[part16(col), :] = sb[part16(col), :]
    out_c[...] = pltpu.roll(made_qo + d_qo, CD, 1)[:, 0:CD]
    dkv_all.wait_send()
    dqo_all.wait_send()
    select_s[...] = onehot(edge_token(iota((TOKENS, 128), 1)) == iota((TOKENS, 128), 0))
    spread = onehot(pooled(iota((TOKENS, 16), 1), iota((TOKENS, 16), 0)))
    dyt[...] = jnp.zeros((WIDTH, HEADS * TOKENS), BF)
    spread_t = onehot(pooled(iota((16, TOKENS), 0), iota((16, TOKENS), 1)))
    lane = iota((CD, HEADS * TOKENS), 1)
    entry = iota((CD, HEADS * TOKENS), 0)
    query = (lane >> 9) * half_size + (lane & (half_size - 1))
    collect = onehot((((lane >> 7) & 3) == (entry >> 4)) & pooled(entry & 15, query))
    sums = []
    for half in range(2):
        lanes = head(half, HEADS * half_size)
        total = [mt(pt[part, lanes].astype(BF), collect[:, lanes]) for part in (OWN, HALF_HALO[half])]
        sums.append(total)
    zeros = jnp.zeros((128, CD), F32)
    halo_sum = jnp.concatenate([sums[0][1], zeros], axis=0) + jnp.concatenate([zeros, sums[1][1]], axis=0)
    share_sum = jnp.concatenate([sums[0][0] + sums[1][0], halo_sum], axis=0)
    high = share_sum.astype(BF)
    low = (share_sum - high.astype(F32)).astype(BF)
    psum[:, 0:CD] = high
    psum[:, CD : 2 * CD] = low
    phase("rs_wait")
    rs_all.wait_recv()
    phase("norm_back")
    grad = rb[0:16, :].astype(F32)
    for c in range(1, NC):
        grad = grad + rb[head(c, 16), :].astype(F32)

    merged = mm_s[...]
    inv_m = inv_s[...]
    grad = inv_m * (grad - merged * (inv_m * inv_m * token_sum(grad * merged) * (1.0 / (4 * WIDTH))))
    dy_blocks = (grad * (1.0 / 16.0)).astype(BF)
    dy_t = mm(mt(eye_s[...], dy_blocks).astype(BF), spread_t)
    dy = mm(spread, dy_blocks)
    by_block = jnp.concatenate([dy_blocks.astype(F32) * head_mask[h] for h in range(HEADS)], axis=0).astype(BF)
    by_block = jnp.concatenate([by_block, by_block], axis=0)

    phase("halo_back")
    d_v = mm(psum[...], by_block)
    spread_heads(dyt, dy_t)
    product = dy_t * fo_s[...]
    by_head = [jnp.sum(product[head(h, CD), :], axis=0, keepdims=True) for h in range(HEADS)]
    delta = [
        jnp.concatenate([by_head[2 * pair + h][:, head(half, half_size)] for h in range(2)], axis=1)
        for half, pair in groups
    ]

    def score_side(part, half):
        values = kvx[part, WIDTH : 2 * WIDTH]
        for pair in range(2):
            lanes = lanes_of(half, pair)
            d_p = mm(values, dyt[:, lanes]) - delta[2 * half + pair]
            ds[part, lanes] = (pt[part, lanes] * d_p).astype(BF)

    def back_copy(k, source, target, i):
        o = OPPOSITE[k]
        source = source.at[pl.ds(START[k], LENGTH[k])]
        target = target.at[pl.ds(START[o], LENGTH[o])]
        return remote(source, target, back_ss.at[i], back_rs.at[i], *neighbour(k))

    def back_k(k):
        return back_copy(k, dk_halo, rh_k, k)

    def back_v(k):
        return back_copy(k, dv_halo, rh_v, 8 + k)

    dv_halo[0:96, :] = d_v[288:384, :].astype(BF)
    dv_halo[96:192, :] = d_v[512:608, :].astype(BF)
    dv_halo[192:320, :] = d_v[384:512, :].astype(BF)
    start_all(back_v)

    upper = slice(0, HEADS * half_size)
    lower = slice(HEADS * half_size, 2 * HEADS * half_size)
    score_side(HALF_HALO[0], 0)
    d_k_upper = mm(ds[HALF_HALO[0], upper], qh[upper, :])
    score_side(HALF_HALO[1], 1)
    d_k_lower = mm(ds[HALF_HALO[1], lower], qh[lower, :])
    dk_halo[192:320, :] = (d_k_upper[128:256, :] + d_k_lower[0:128, :]).astype(BF)
    dk_halo[0:96, :] = d_k_upper[32:128, :].astype(BF)
    dk_halo[96:192, :] = d_k_lower[128:224, :].astype(BF)
    start_all(back_k)

    phase("own_back")
    score_side(OWN, 0)
    score_side(OWN, 1)
    d_k = mm(ds[OWN, :], qh[...])
    d_v = d_v[OWN, :]
    phase("query_back")
    pieces = []
    for half, pair in groups:
        lanes = lanes_of(half, pair)
        from_own = mm(kt[head(pair, 2 * CD), OWN], ds[OWN, lanes])
        from_halo = mm(kt[head(pair, 2 * CD), HALF_HALO[half]], ds[HALF_HALO[half], lanes])
        pieces.append(from_own + from_halo)
    d_q = transposed(join_heads(pieces).astype(BF))
    raw_q = rq_s[...]
    inv_q = iq_s[...]
    g_q = gain * inv_q * (d_q - raw_q * (inv_q * inv_q * mm((d_q * raw_q).astype(BF), blocks)))
    result = dy + mm(g_q.astype(BF), fproj_t[0:WIDTH, :])
    rs_all.wait_send()

    phase("back_wait")
    for k in range(8):
        back_v(OPPOSITE[k]).wait_recv()

    def received(ref):
        rows = [ref[0:96, :].astype(F32), jnp.zeros((TOKENS - 192, WIDTH), F32), ref[96:192, :].astype(F32)]
        return mm(select_s[...], ref[192:320, :]) + jnp.concatenate(rows, axis=0)

    d_v = d_v + received(rh_v)
    result = result + mm(d_v.astype(BF), fproj_t[2 * WIDTH :, :])
    for k in range(8):
        back_k(OPPOSITE[k]).wait_recv()
    phase("finish")
    d_k = d_k + received(rh_k)
    raw_k = rk_s[...]
    inv_k = ik_s[...]
    g_k = inv_k * (d_k - raw_k * (inv_k * inv_k * mm((d_k * raw_k).astype(BF), blocks)))
    result = result + mm(g_k.astype(BF), fproj_t[WIDTH : 2 * WIDTH, :])
    out_f[...] = result.astype(BF)
    for k in range(8):
        back_v(k).wait_send()
        back_k(k).wait_send()
    open_scope.close()


def in_hbm(x):
    return pltpu.with_memory_space_constraint(x, pltpu.HBM)


def body(tokens, fine_proj, fine_scale, coarse_proj, coarse_scale, coarse_cot):
    vmem = pl.BlockSpec(memory_space=pltpu.VMEM)
    smem = pl.BlockSpec(memory_space=pltpu.SMEM)
    hbm = pl.BlockSpec(memory_space=pltpu.HBM)
    dma = pltpu.SemaphoreType.DMA
    out_c, out_f = pl.pallas_call(
        kernel,
        out_shape=(
            jax.ShapeDtypeStruct((CT, CD), F32),
            jax.ShapeDtypeStruct((TOKENS, WIDTH), BF),
        ),
        in_specs=[hbm, hbm, hbm, hbm, smem, hbm],
        out_specs=(vmem, vmem),
        scratch_shapes=[
            pltpu.VMEM((TOKENS, WIDTH), BF),
            pltpu.VMEM((WIDTH, 3 * WIDTH), BF),
            pltpu.SMEM((HEADS,), F32),
            pltpu.VMEM((CT, CD), BF),
            pltpu.VMEM((KEYS, 2 * WIDTH), BF),
            pltpu.VMEM((128, 2 * WIDTH), BF),
            pltpu.VMEM((TOKENS, WIDTH), F32),
            pltpu.VMEM((TOKENS, WIDTH), F32),
            pltpu.VMEM((TOKENS, WIDTH), F32),
            pltpu.VMEM((TOKENS, WIDTH), F32),
            pltpu.VMEM((HEADS * TOKENS, WIDTH), BF),
            pltpu.VMEM((WIDTH, HEADS * TOKENS), BF),
            pltpu.VMEM((KEYS, HEADS * TOKENS), F32),
            pltpu.VMEM((KEYS, 2 * CD), BF),
            pltpu.VMEM((2 * WIDTH, TOKENS), F32),
            pltpu.VMEM((TOKENS, WIDTH), F32),
            pltpu.VMEM((WIDTH, KEYS), BF),
            pltpu.VMEM((3 * WIDTH, WIDTH), BF),
            pltpu.VMEM((4 * CD, 4 * WIDTH), BF),
            pltpu.VMEM((4 * WIDTH, 4 * CD), BF),
            pltpu.VMEM((16 * NC, WIDTH), BF),
            pltpu.VMEM((16, WIDTH), F32),
            pltpu.VMEM((16, 1), F32),
            pltpu.VMEM((WIDTH, WIDTH), BF),
            pltpu.VMEM((8 * CD, WIDTH), BF),
            pltpu.VMEM((8 * CD, WIDTH), BF),
            pltpu.VMEM((TOKENS, 128), BF),
            pltpu.VMEM((NZ * CT, 2 * CD), BF),
            pltpu.VMEM((NM * CT, 2 * CD), BF),
            pltpu.VMEM((NM, 2, NM * CT), F32),
            pltpu.VMEM((NZ * CT, NM * CT), F32),
            pltpu.VMEM((NZ * CT, NM * CT), F32),
            pltpu.VMEM((NZ * CT, NM * CT), BF),
            pltpu.VMEM((NZ * CT, 2 * CD), BF),
            pltpu.VMEM((NZ * CT, 2 * CD), BF),
            pltpu.VMEM((NM * CT, 2 * CD), BF),
            pltpu.VMEM((NM * CT, 2 * CD), BF),
            pltpu.VMEM((16 * NC, WIDTH), BF),
            pltpu.VMEM((16 * NC, WIDTH), BF),
            pltpu.VMEM((WIDTH, HEADS * TOKENS), BF),
            pltpu.VMEM((KEYS, HEADS * TOKENS), BF),
            pltpu.VMEM((HALO, WIDTH), BF),
            pltpu.VMEM((HALO, WIDTH), BF),
            pltpu.VMEM((HALO, WIDTH), BF),
            pltpu.VMEM((HALO, WIDTH), BF),
            dma((4,)), dma((3,)), dma((8,)), dma((8,)),
            dma(()), dma(()), dma(()), dma((NZ,)), dma(()), dma(()), dma(()), dma(()),
            dma(()), dma(()), dma(()), dma(()), dma(()), dma(()),
            dma((16,)), dma((16,)),
        ],
        compiler_params=pltpu.CompilerParams(
            collective_id=0, has_side_effects=True, vmem_limit_bytes=40 * 1024 * 1024
        ),
        cost_estimate=pl.CostEstimate(
            flops=3_000_000_000, bytes_accessed=2_000_000, transcendentals=1_000_000
        ),
        name="hourglass",
    )(
        in_hbm(tokens.reshape(TOKENS, WIDTH)),
        in_hbm(fine_proj),
        in_hbm(fine_scale),
        in_hbm(jnp.swapaxes(coarse_proj, 1, 2)),
        coarse_scale,
        in_hbm(coarse_cot.reshape(CT, CD)),
    )
    return out_c.reshape(1, CT, CD), out_f.reshape(ROWS, COLS, WIDTH)


def solution(mesh):
    return jax.shard_map(
        body,
        mesh=mesh,
        in_specs=(
            P("row", "col", None),
            P(),
            P(),
            P(None, None, "col"),
            P("col"),
            P("row", None, "col"),
        ),
        out_specs=(P("row", None, "col"), P("row", "col", None)),
        check_vma=False,
    )
```

time: 558 us -> 62.3 us (0.11); the launches traced: 549 us -> 62.2 us
  blocking collectives: 251 us -> 0 us
  waiting for transfers between devices: 153 us -> 0 us
  Pallas kernels: 0 us -> 59.6 us
  local copies, waits for them, and re-layouts: 58.1 us -> 1.27 us
  starting transfers between devices: 35.5 us -> 0 us
  matrix products: 19.7 us -> 0 us
  between operations: 17.2 us -> 1.29 us
  other arithmetic: 14.8 us -> 0 us
    all_gather x5 -> x0, blocking collectives: 197 us -> none  [the longest x1 43.3 us: body(): lax.all_gather(coarse_key, 'row', axis=0, tiled=True)]
    unnamed x2 -> x0, waiting for transfers between devices: 152 us -> none
    pallas_call x0 -> x1, Pallas kernels: none -> 59.6 us  [body(): pl.pallas_call(kernel, out_shape=(jax.ShapeDtypeStruct((CT, CD), F32), ja...]
    unnamed x1 -> x0, blocking collectives: 54.1 us -> none
    ppermute x8 -> x0, starting transfers between devices: 35.5 us -> none  [the longest x4 22 us: shifted(): lax.ppermute(value, axis, [(source, source + steps) for source in range(f...]
    dot_general x15 -> x0, matrix products: 19.5 us -> none  [the longest x1 2.75 us: body(): jnp.einsum('thqk,tqhd->tkhd', shares.astype(jnp.bfloat16), cot_block, pre...]
    unnamed x108 -> x2, local copies, waits for them, and re-layouts: 13.2 us -> 1.27 us
    all_gather x3 -> x0, local copies, waits for them, and re-layouts: 10.2 us -> none  [the longest x1 3.46 us: body(): lax.all_gather(coarse_value, 'row', axis=0, tiled=True)]
  transfers between devices with their start and end apart: 9 -> 0, of which waited for: 2 -> 0; matrix products, arithmetic and copies ran while one was open for 3% -> 0% of each run, Pallas kernels for 0% -> 0%
where the time goes in v1:
time: 62.3 us; the launch traced here: 62.2 us
  Pallas kernels  59.6 us (96%)
  between operations  1.29 us (2%)
  local copies, waits for them, and re-layouts  1.27 us (2%)
    pallas_call x1, Pallas kernels, body(): pl.pallas_call(kernel, out_shape=(jax.ShapeDtypeStruct((CT, CD), F32), ja...  59.6 us
    unnamed x2, local copies, waits for them, and re-layouts  1.27 us

profile of v1, /device:TPU:1, one launch (start us, length us, event | category | flops | bytes accessed | tf_op | source)
XLA Modules:
  0.0 62.2 jit_solution(2401227995137732374)
XLA Ops:
  1.3 59.6 %hourglass.1 = (f32[64,64]{1,0:T(8,128)S(1)}, bf16[256,256]{1,0:T(8,128)(2,1)S(1)}) custom-call(bf16[256,256]{1,0:T(8,128)(2,1)} %bitcast.8, bf16[256,768]{1,0:T(8,128)(2,1)} %fproj_hbm.1, f32[4]{0:T(128)} %fscale_hbm.1, bf16[3,64,1024]{2,1,0:T(8,128)(2,1)} %bitcast.7, f32[1]{0:T(128)S(6)} %copy.10.cscale, bf16[64,64]{1,0:T(8,128)(2,1)} %bitcast.9), custom_call_target="tpu_custom_call" | custom-call | flops 3000000000 | bytes 2000000 | tf_op jit(solution)/shard_map/hourglass/pallas_call | solution.py:658
  60.9 0.6 copy.11
  61.5 0.7 %copy.12 = bf16[8,32,256]{2,1,0:T(8,128)(2,1)} copy(bf16[8,32,256]{2,1,0:T(8,128)(2,1)S(1)} %bitcast.5) | data formatting | bytes 262144

commit v2 on v1

--- a/solution.py
+++ b/solution.py
@@ -66,9 +66,9 @@
 def kernel(
     tok_hbm, fproj_hbm, fscale_hbm, cproj, cscale, cot_hbm,
     out_c, out_f,
-    tok, fproj, fscale, cot, kvx, staging, rq_s, rk_s, iq_s, ik_s, qh, qt, pt, psum, fot, fo_s, kt, fproj_t, wxt, wide, cg, mm_s, inv_s,
+    tok, fproj, fscale, cot, kvx, halo_tok, staging, rq_s, rk_s, iq_s, ik_s, qh, qt, pt, psum, fot, fo_s, kt, fproj_t, wxt, wide, cg, mm_s, inv_s,
     eye_s, w_kv, w_qc, select_s,
-    kv, qc, st, ce_s, dp_s, cds_s, dkv, dkv_in, dqo, dqo_in, sb, rb, dyt, ds, dk_halo, dv_halo, rh_k, rh_v,
+    kv, qc, st, ce_s, dp_s, cds_s, dkv, dkv_in, dqo, dqo_in, sb, rb, dyt, ds, dg_halo, rh,
     in_sem, w_sem, halo_ss, halo_rs, cg_ss, cg_rs, kv_ss, kv_rs, qc_ss, qc_rs, st_ss, st_rs,
     dkv_ss, dkv_rs, dqo_ss, dqo_rs, rs_ss, rs_rs, back_ss, back_rs,
 ):
@@ -136,38 +136,20 @@
         greet(index_of(m, z), col)
 
     phase("inputs_wait")
-    lane = iota((1, WIDTH), 1)
-    head_mask = [jnp.where((lane >> 6) == h, 1.0, 0.0) for h in range(HEADS)]
-    blocks = onehot((iota((WIDTH, WIDTH), 0) >> 6) == (iota((WIDTH, WIDTH), 1) >> 6))
-    for c in copies[0:2]:
-        c.wait()
-    for c in weight_copies:
-        c.start()
-    phase("projection")
-    token = tok[...]
-    raw_k = mm(token, fproj[:, WIDTH : 2 * WIDTH])
-    inv_k = lax.rsqrt(mm((raw_k * raw_k).astype(BF), blocks) + EPS)
-    unit_k = (raw_k * inv_k).astype(BF)
-    value = mm(token, fproj[:, 2 * WIDTH :]).astype(BF)
-    kvx[OWN, 0:WIDTH] = unit_k
-    kvx[OWN, WIDTH : 2 * WIDTH] = value
-    kvx[256:288, :] = jnp.zeros((32, 2 * WIDTH), BF)
-    kvx[608:640, :] = jnp.zeros((32, 2 * WIDTH), BF)
-
     def edge_token(slot):
         side, down, across, right, bottom, used = edge_parts(slot)
         return jnp.where(used, (down + 5 * bottom) * COLS + across + (COLS - 3) * right, -1)
 
     select = onehot(edge_token(iota((128, TOKENS), 0)) == iota((128, TOKENS), 1))
-    staging[:, 0:WIDTH] = mm(select, unit_k).astype(BF)
-    staging[:, WIDTH : 2 * WIDTH] = mm(select, value).astype(BF)
-    rk_s[...] = raw_k
-    ik_s[...] = inv_k
-
+    copies[0].wait()
+    token = tok[...]
+    staging[...] = mm(select, token).astype(BF)
+    nothing = jnp.zeros((32, WIDTH), BF)
+    halo_tok[0:32, :] = nothing
+    halo_tok[KEYS - TOKENS - 32 :, :] = nothing
     phase("barrier_wait")
     pl.semaphore_wait(barrier, len(col_peers) + len(z_peers) + len(mates) + 5)
 
-    phase("halo_send")
     def remote(src, dst, ss, rs, r, c):
         return pltpu.make_async_remote_copy(
             src_ref=src, dst_ref=dst, send_sem=ss, recv_sem=rs, device_id=(r, c), device_id_type=MESH
@@ -176,33 +158,36 @@
     def halo_copy(k):
         o = OPPOSITE[k]
         if k == 0:
-            source = kvx.at[pl.ds(OWN.start, 96)]
+            source = tok.at[pl.ds(0, 96)]
         elif k == 1:
-            source = kvx.at[pl.ds(OWN.stop - 96, 96)]
+            source = tok.at[pl.ds(TOKENS - 96, 96)]
         else:
             source = staging.at[pl.ds(START[k] - 192, LENGTH[k])]
-        target = kvx.at[pl.ds(PLACE[o], LENGTH[o])]
+        target = halo_tok.at[pl.ds(PLACE[o] - TOKENS, LENGTH[o])]
         return remote(source, target, halo_ss.at[k], halo_rs.at[k], *neighbour(k))
 
-    def start_all(copy):
-        for k in (4, 5, 6, 7, 2, 3):
-            copy(k).start()
-
-        @pl.when(core == 0)
-        def _():
-            copy(0).start()
-            copy(1).start()
-
-        @pl.when(core == 1)
-        def _():
-            copy(1).start()
-            copy(0).start()
-
-    start_all(halo_copy)
+    for k in (4, 5, 6, 7, 2, 3, 0, 1):
+        halo_copy(k).start()
 
     phase("own_attend")
-    for c in copies[2:4]:
+    for c in copies[1:4]:
         c.wait()
+    for c in weight_copies:
+        c.start()
+    lane = iota((1, WIDTH), 1)
+    head_mask = [jnp.where((lane >> 6) == h, 1.0, 0.0) for h in range(HEADS)]
+    blocks = onehot((iota((WIDTH, WIDTH), 0) >> 6) == (iota((WIDTH, WIDTH), 1) >> 6))
+
+    def project(x):
+        raw = mm(x, fproj[:, WIDTH : 2 * WIDTH])
+        inv = lax.rsqrt(mm((raw * raw).astype(BF), blocks) + EPS)
+        return raw, inv, mm(x, fproj[:, 2 * WIDTH :]).astype(BF)
+
+    raw_k, inv_k, value = project(token)
+    kvx[OWN, 0:WIDTH] = (raw_k * inv_k).astype(BF)
+    kvx[OWN, WIDTH : 2 * WIDTH] = value
+    rk_s[...] = raw_k
+    ik_s[...] = inv_k
     gain = sum(head_mask[h] * fscale[h] for h in range(HEADS))
     raw_q = mm(token, fproj[:, 0:WIDTH])
     inv_q = lax.rsqrt(mm((raw_q * raw_q).astype(BF), blocks) + EPS)
@@ -300,7 +285,10 @@
         halo_copy(OPPOSITE[k]).wait_recv()
 
     phase("halo_attend")
-    halo_t = transposed(kvx[TOKENS:KEYS, WIDTH : 2 * WIDTH]).astype(BF)
+    raw_halo, inv_halo, halo_value = project(halo_tok[...])
+    kvx[TOKENS:KEYS, 0:WIDTH] = (raw_halo * inv_halo).astype(BF)
+    kvx[TOKENS:KEYS, WIDTH : 2 * WIDTH] = halo_value
+    halo_t = transposed(halo_value).astype(BF)
     linv, outs_all = [], []
     for half in range(2):
         halo_values = halo_t[:, half * 128 : half * 128 + 256]
@@ -558,7 +546,6 @@
     by_block = jnp.concatenate([by_block, by_block], axis=0)
 
     phase("halo_back")
-    d_v = mm(psum[...], by_block)
     spread_heads(dyt, dy_t)
     product = dy_t * fo_s[...]
     by_head = [jnp.sum(product[head(h, CD), :], axis=0, keepdims=True) for h in range(HEADS)]
@@ -574,22 +561,16 @@
             d_p = mm(values, dyt[:, lanes]) - delta[2 * half + pair]
             ds[part, lanes] = (pt[part, lanes] * d_p).astype(BF)
 
-    def back_copy(k, source, target, i):
+    d_v = mm(psum[...], by_block)
+    dg_halo[0:96, WIDTH : 2 * WIDTH] = d_v[288:384, :].astype(BF)
+    dg_halo[96:192, WIDTH : 2 * WIDTH] = d_v[512:608, :].astype(BF)
+    dg_halo[192:320, WIDTH : 2 * WIDTH] = d_v[384:512, :].astype(BF)
+
+    def back_copy(k):
         o = OPPOSITE[k]
-        source = source.at[pl.ds(START[k], LENGTH[k])]
-        target = target.at[pl.ds(START[o], LENGTH[o])]
-        return remote(source, target, back_ss.at[i], back_rs.at[i], *neighbour(k))
-
-    def back_k(k):
-        return back_copy(k, dk_halo, rh_k, k)
-
-    def back_v(k):
-        return back_copy(k, dv_halo, rh_v, 8 + k)
-
-    dv_halo[0:96, :] = d_v[288:384, :].astype(BF)
-    dv_halo[96:192, :] = d_v[512:608, :].astype(BF)
-    dv_halo[192:320, :] = d_v[384:512, :].astype(BF)
-    start_all(back_v)
+        source = dg_halo.at[pl.ds(START[k], LENGTH[k])]
+        target = rh.at[pl.ds(START[o], LENGTH[o])]
+        return remote(source, target, back_ss.at[k], back_rs.at[k], *neighbour(k))
 
     upper = slice(0, HEADS * half_size)
     lower = slice(HEADS * half_size, 2 * HEADS * half_size)
@@ -597,10 +578,13 @@
     d_k_upper = mm(ds[HALF_HALO[0], upper], qh[upper, :])
     score_side(HALF_HALO[1], 1)
     d_k_lower = mm(ds[HALF_HALO[1], lower], qh[lower, :])
-    dk_halo[192:320, :] = (d_k_upper[128:256, :] + d_k_lower[0:128, :]).astype(BF)
-    dk_halo[0:96, :] = d_k_upper[32:128, :].astype(BF)
-    dk_halo[96:192, :] = d_k_lower[128:224, :].astype(BF)
-    start_all(back_k)
+    dg_halo[192:320, 0:WIDTH] = (d_k_upper[128:256, :] + d_k_lower[0:128, :]).astype(BF)
+    for k in (4, 5, 6, 7, 2, 3):
+        back_copy(k).start()
+    dg_halo[0:96, 0:WIDTH] = d_k_upper[32:128, :].astype(BF)
+    back_copy(0).start()
+    dg_halo[96:192, 0:WIDTH] = d_k_lower[128:224, :].astype(BF)
+    back_copy(1).start()
 
     phase("own_back")
     score_side(OWN, 0)
@@ -623,26 +607,26 @@
 
     phase("back_wait")
     for k in range(8):
-        back_v(OPPOSITE[k]).wait_recv()
-
-    def received(ref):
-        rows = [ref[0:96, :].astype(F32), jnp.zeros((TOKENS - 192, WIDTH), F32), ref[96:192, :].astype(F32)]
-        return mm(select_s[...], ref[192:320, :]) + jnp.concatenate(rows, axis=0)
-
-    d_v = d_v + received(rh_v)
-    result = result + mm(d_v.astype(BF), fproj_t[2 * WIDTH :, :])
-    for k in range(8):
-        back_k(OPPOSITE[k]).wait_recv()
+        back_copy(OPPOSITE[k]).wait_recv()
     phase("finish")
-    d_k = d_k + received(rh_k)
+    received = mm(select_s[...], rh[192:320, :]) + jnp.concatenate(
+        [
+            rh[0:96, :].astype(F32),
+            jnp.zeros((TOKENS - 192, 2 * WIDTH), F32),
+            rh[96:192, :].astype(F32),
+        ],
+        axis=0,
+    )
+    d_k = d_k + received[:, 0:WIDTH]
+    d_v = d_v + received[:, WIDTH : 2 * WIDTH]
     raw_k = rk_s[...]
     inv_k = ik_s[...]
     g_k = inv_k * (d_k - raw_k * (inv_k * inv_k * mm((d_k * raw_k).astype(BF), blocks)))
-    result = result + mm(g_k.astype(BF), fproj_t[WIDTH : 2 * WIDTH, :])
+    g_kv = jnp.concatenate([g_k.astype(BF), d_v.astype(BF)], axis=1)
+    result = result + mm(g_kv, fproj_t[WIDTH:, :])
     out_f[...] = result.astype(BF)
     for k in range(8):
-        back_v(k).wait_send()
-        back_k(k).wait_send()
+        back_copy(k).wait_send()
     open_scope.close()
 
 
@@ -669,7 +653,8 @@
             pltpu.SMEM((HEADS,), F32),
             pltpu.VMEM((CT, CD), BF),
             pltpu.VMEM((KEYS, 2 * WIDTH), BF),
-            pltpu.VMEM((128, 2 * WIDTH), BF),
+            pltpu.VMEM((KEYS - TOKENS, WIDTH), BF),
+            pltpu.VMEM((128, WIDTH), BF),
             pltpu.VMEM((TOKENS, WIDTH), F32),
             pltpu.VMEM((TOKENS, WIDTH), F32),
             pltpu.VMEM((TOKENS, WIDTH), F32),
@@ -705,14 +690,12 @@
             pltpu.VMEM((16 * NC, WIDTH), BF),
             pltpu.VMEM((WIDTH, HEADS * TOKENS), BF),
             pltpu.VMEM((KEYS, HEADS * TOKENS), BF),
-            pltpu.VMEM((HALO, WIDTH), BF),
-            pltpu.VMEM((HALO, WIDTH), BF),
-            pltpu.VMEM((HALO, WIDTH), BF),
-            pltpu.VMEM((HALO, WIDTH), BF),
+            pltpu.VMEM((HALO, 2 * WIDTH), BF),
+            pltpu.VMEM((HALO, 2 * WIDTH), BF),
             dma((4,)), dma((3,)), dma((8,)), dma((8,)),
             dma(()), dma(()), dma(()), dma((NZ,)), dma(()), dma(()), dma(()), dma(()),
             dma(()), dma(()), dma(()), dma(()), dma(()), dma(()),
-            dma((16,)), dma((16,)),
+            dma((8,)), dma((8,)),
         ],
         compiler_params=pltpu.CompilerParams(
             collective_id=0, has_side_effects=True, vmem_limit_bytes=40 * 1024 * 1024

time: 62.3 us -> 61.1 us (0.981)
  Pallas kernels: 59.6 us -> 58.4 us
    pallas_call x1, Pallas kernels: 59.6 us -> 58.4 us  [body(): pl.pallas_call(kernel, out_shape=(jax.ShapeDtypeStruct((CT, CD), F32), ja...]
where the time goes in v2:
time: 61.1 us; the launch traced here: 61 us
  Pallas kernels  58.4 us (96%)
  between operations  1.29 us (2%)
  local copies, waits for them, and re-layouts  1.27 us (2%)
    pallas_call x1, Pallas kernels, body(): pl.pallas_call(kernel, out_shape=(jax.ShapeDtypeStruct((CT, CD), F32), ja...  58.4 us
    unnamed x2, local copies, waits for them, and re-layouts  1.27 us

profile of v2, /device:TPU:1, one launch (start us, length us, event | category | flops | bytes accessed | tf_op | source)
XLA Modules:
  0.0 61.0 jit_solution(18306449249305891198)
XLA Ops:
  1.3 58.4 %hourglass.1 = (f32[64,64]{1,0:T(8,128)S(1)}, bf16[256,256]{1,0:T(8,128)(2,1)S(1)}) custom-call(bf16[256,256]{1,0:T(8,128)(2,1)} %bitcast.8, bf16[256,768]{1,0:T(8,128)(2,1)} %fproj_hbm.1, f32[4]{0:T(128)} %fscale_hbm.1, bf16[3,64,1024]{2,1,0:T(8,128)(2,1)} %bitcast.7, f32[1]{0:T(128)S(6)} %copy.10.cscale, bf16[64,64]{1,0:T(8,128)(2,1)} %bitcast.9), custom_call_target="tpu_custom_call" | custom-call | flops 3000000000 | bytes 2000000 | tf_op jit(solution)/shard_map/hourglass/pallas_call | solution.py:642
  59.7 0.6 %copy.11 = f32[1,64,64]{2,1,0:T(8,128)} copy(f32[1,64,64]{2,1,0:T(8,128)S(1)} %bitcast.6) | data formatting | bytes 32768
  60.3 0.7 %copy.12 = bf16[8,32,256]{2,1,0:T(8,128)(2,1)} copy(bf16[8,32,256]{2,1,0:T(8,128)(2,1)S(1)} %bitcast.5) | data formatting | bytes 262144

commit v3 on v2

--- a/solution.py
+++ b/solution.py
@@ -106,6 +106,16 @@
 
     def greet(r, c):
         pl.semaphore_signal(barrier, inc=1, device_id=(r, c), device_id_type=MESH)
+
+    def when_inside(k, action):
+        r, c = row + DIRS[k][0], col + DIRS[k][1]
+
+        @pl.when((r >= 0) & (r < NR) & (c >= 0) & (c < NC))
+        def _():
+            action(k)
+
+    halo_tok[...] = jnp.zeros((KEYS - TOKENS, WIDTH), BF)
+    rh[...] = jnp.zeros((HALO, 2 * WIDTH), BF)
 
     phase("greet")
     for c in col_peers[0:9]:
@@ -144,9 +154,6 @@
     copies[0].wait()
     token = tok[...]
     staging[...] = mm(select, token).astype(BF)
-    nothing = jnp.zeros((32, WIDTH), BF)
-    halo_tok[0:32, :] = nothing
-    halo_tok[KEYS - TOKENS - 32 :, :] = nothing
     phase("barrier_wait")
     pl.semaphore_wait(barrier, len(col_peers) + len(z_peers) + len(mates) + 5)
 
@@ -167,7 +174,7 @@
         return remote(source, target, halo_ss.at[k], halo_rs.at[k], *neighbour(k))
 
     for k in (4, 5, 6, 7, 2, 3, 0, 1):
-        halo_copy(k).start()
+        when_inside(k, lambda k: halo_copy(k).start())
 
     phase("own_attend")
     for c in copies[1:4]:
@@ -282,7 +289,7 @@
 
     phase("halo_wait")
     for k in range(8):
-        halo_copy(OPPOSITE[k]).wait_recv()
+        when_inside(k, lambda k: halo_copy(OPPOSITE[k]).wait_recv())
 
     phase("halo_attend")
     raw_halo, inv_halo, halo_value = project(halo_tok[...])
@@ -348,7 +355,7 @@
         for part in (OWN, HALF_HALO[half]):
             pt[part, lanes] = pt[part, lanes] * linv[2 * half + pair]
     for k in range(8):
-        halo_copy(k).wait_send()
+        when_inside(k, lambda k: halo_copy(k).wait_send())
     phase("cn_wait")
     cg_all.wait_recv()
 
@@ -580,11 +587,11 @@
     d_k_lower = mm(ds[HALF_HALO[1], lower], qh[lower, :])
     dg_halo[192:320, 0:WIDTH] = (d_k_upper[128:256, :] + d_k_lower[0:128, :]).astype(BF)
     for k in (4, 5, 6, 7, 2, 3):
-        back_copy(k).start()
+        when_inside(k, lambda k: back_copy(k).start())
     dg_halo[0:96, 0:WIDTH] = d_k_upper[32:128, :].astype(BF)
-    back_copy(0).start()
+    when_inside(0, lambda k: back_copy(k).start())
     dg_halo[96:192, 0:WIDTH] = d_k_lower[128:224, :].astype(BF)
-    back_copy(1).start()
+    when_inside(1, lambda k: back_copy(k).start())
 
     phase("own_back")
     score_side(OWN, 0)
@@ -607,7 +614,7 @@
 
     phase("back_wait")
     for k in range(8):
-        back_copy(OPPOSITE[k]).wait_recv()
+        when_inside(k, lambda k: back_copy(OPPOSITE[k]).wait_recv())
     phase("finish")
     received = mm(select_s[...], rh[192:320, :]) + jnp.concatenate(
         [
@@ -626,7 +633,7 @@
     result = result + mm(g_kv, fproj_t[WIDTH:, :])
     out_f[...] = result.astype(BF)
     for k in range(8):
-        back_copy(k).wait_send()
+        when_inside(k, lambda k: back_copy(k).wait_send())
     open_scope.close()
 
 

time: 61.1 us -> 58.2 us (0.953)
  Pallas kernels: 58.4 us -> 55.5 us
    pallas_call x1, Pallas kernels: 58.4 us -> 55.5 us  [body(): pl.pallas_call(kernel, out_shape=(jax.ShapeDtypeStruct((CT, CD), F32), ja...]
where the time goes in v3:
time: 58.2 us; the launch traced here: 58 us
  Pallas kernels  55.5 us (95%)
  between operations  1.29 us (2%)
  local copies, waits for them, and re-layouts  1.27 us (2%)
    pallas_call x1, Pallas kernels, body(): pl.pallas_call(kernel, out_shape=(jax.ShapeDtypeStruct((CT, CD), F32), ja...  55.5 us
    unnamed x2, local copies, waits for them, and re-layouts  1.27 us

profile of v3, /device:TPU:1, one launch (start us, length us, event | category | flops | bytes accessed | tf_op | source)
XLA Modules:
  0.0 58.0 jit_solution(9088756153063868264)
XLA Ops:
  1.3 55.5 %hourglass.1 = (f32[64,64]{1,0:T(8,128)S(1)}, bf16[256,256]{1,0:T(8,128)(2,1)S(1)}) custom-call(bf16[256,256]{1,0:T(8,128)(2,1)} %bitcast.8, bf16[256,768]{1,0:T(8,128)(2,1)} %fproj_hbm.1, f32[4]{0:T(128)} %fscale_hbm.1, bf16[3,64,1024]{2,1,0:T(8,128)(2,1)} %bitcast.7, f32[1]{0:T(128)S(6)} %copy.10.cscale, bf16[64,64]{1,0:T(8,128)(2,1)} %bitcast.9), custom_call_target="tpu_custom_call" | custom-call | flops 3000000000 | bytes 2000000 | tf_op jit(solution)/shard_map/hourglass/pallas_call | solution.py:649
  56.7 0.6 %copy.11 = f32[1,64,64]{2,1,0:T(8,128)} copy(f32[1,64,64]{2,1,0:T(8,128)S(1)} %bitcast.6) | data formatting | bytes 32768
  57.4 0.7 %copy.12 = bf16[8,32,256]{2,1,0:T(8,128)(2,1)} copy(bf16[8,32,256]{2,1,0:T(8,128)(2,1)S(1)} %bitcast.5) | data formatting | bytes 262144
